TPU v7x, 256 devices: a whole 4x4x8 slice. The times are simulated.
256 devices in a mesh: ctx: 16 (over z, core), row: 4 (over x), col: 4 (over y).
Axes of the slice: x: 4, y: 4, z: 8, core: 2. Of those that a mesh axis runs over, the one named last changes fastest.
Arguments:
- projected: bfloat16 [16384, 8704], P(('ctx', 'row'), 'col'), may hold values from -6 to 6
- conv_taps: float32 [3, 8704], P(None, 'col'), may hold values from -3 to 3
- out_weight: bfloat16 [8192, 8192], P('col', 'row'), may hold values from -0.0625 to 0.0625
Outputs:
- output: bfloat16 [16384, 8192], P(('ctx', 'col'), 'row')
All inputs are finite; a program needn't handle non-finite values.
Results may differ from a plain program's by a relative error of at most 0.02.
Values may be sent and summed in bfloat16 or wider, within the bound.
A program may use at most 192 MiB of HBM per device.

v0:
```python
import jax
import jax.numpy as jnp
import numpy as np
from jax import lax
from jax.sharding import PartitionSpec as P

FEAT = 16
DV = 512
PHI = 153


def from_behind(value, axis, by):
    length = lax.axis_size(axis)
    pairs = [(i, i + by) for i in range(length) if 0 <= i + by < length]
    return lax.ppermute(value, axis, pairs)


def entering(value, axis, join, neutral):
    place = lax.axis_index(axis)
    gathered = jax.tree.map(
        lambda a, kind: lax.all_gather(a.astype(kind), axis),
        value,
        jax.tree.map(lambda a: jnp.bfloat16 if a.dtype == jnp.float32 else a.dtype, value),
    )
    state = jax.tree.map(lambda a, e: jnp.zeros_like(a) + jnp.asarray(e, a.dtype), value, neutral)

    def one(step, state):
        return join(
            state,
            jax.tree.map(
                lambda a, own: lax.dynamic_index_in_dim(a, step, 0, False).astype(own.dtype),
                gathered,
                value,
            ),
        )

    return lax.fori_loop(0, place, one, state)


def features(values):
    width = values.shape[-1]
    first, second = np.triu_indices(width)
    coef = np.where(first == second, (2.0 * width) ** (-0.5), width ** (-0.5)).astype(np.float32)
    ones = jnp.ones(values.shape[:-1] + (1,), values.dtype)
    quad = values[..., first] * values[..., second] * coef
    return jnp.concatenate([ones, values * width ** (-0.25), quad], axis=-1)


def combine(earlier, later):
    return (earlier[0] + later[0], earlier[1] + later[1])


def shards(projected, conv_taps, out_weight):
    width = 2 * FEAT + DV
    heads = projected.shape[1] // width
    rows = projected.shape[0]
    tail = from_behind(projected[-2:], ("ctx", "row"), 1)
    extended = jnp.concatenate([tail, projected], axis=0).astype(jnp.float32)
    convolved = (
        conv_taps[0] * extended[2:] + conv_taps[1] * extended[1:-1] + conv_taps[2] * extended[:-2]
    )
    gated = (extended[2:] * convolved).astype(jnp.bfloat16).reshape(rows, heads, width)
    query = gated[..., :FEAT]
    key = gated[..., FEAT : 2 * FEAT]
    value = gated[..., 2 * FEAT :]
    causal = jnp.arange(rows)[:, None] >= jnp.arange(rows)[None, :]
    scores = jnp.einsum("thi,shi->hts", query, key, preferred_element_type=jnp.float32) * FEAT ** (
        -0.5
    )
    kernel = jnp.where(causal[None], 1.0 + scores + 0.5 * scores * scores, 0.0).astype(jnp.bfloat16)
    num_in = jnp.einsum("hts,shd->thd", kernel, value, preferred_element_type=jnp.float32)
    den_in = jnp.sum(kernel.astype(jnp.float32), axis=-1).T
    value_wide = value.astype(jnp.float32)
    phi_query = features(query.astype(jnp.float32))
    phi_key = features(key.astype(jnp.float32))
    local_num = jnp.einsum(
        "thf,thd->fhd", phi_key, value_wide, precision=lax.Precision.HIGHEST
    ).reshape(PHI, heads * DV)
    local_den = jnp.sum(phi_key, axis=0)
    zero_num = jnp.zeros((PHI, heads * DV), jnp.float32)
    zero_den = jnp.zeros((heads, PHI), jnp.float32)
    group_num, group_den = (
        lax.psum(local_num.astype(jnp.bfloat16), "row").astype(jnp.float32),
        lax.psum(local_den.astype(jnp.bfloat16), "row").astype(jnp.float32),
    )
    inner_num, inner_den = entering((local_num, local_den), "row", combine, (zero_num, zero_den))
    position = lax.axis_index("ctx")
    pieces = (
        lax.all_gather(group_num[None].astype(jnp.bfloat16), "ctx", axis=0, tiled=True).astype(
            jnp.float32
        ),
        lax.all_gather(group_den[None].astype(jnp.bfloat16), "ctx", axis=0, tiled=True).astype(
            jnp.float32
        ),
    )
    keep = jnp.arange(pieces[0].shape[0], dtype=jnp.int32) < position
    summed_num = jnp.sum(jnp.where(keep[:, None, None], pieces[0], 0.0), axis=0)
    summed_den = jnp.sum(jnp.where(keep[:, None, None], pieces[1], 0.0), axis=0)
    outer_num = zero_num + summed_num
    outer_den = zero_den + summed_den
    prior_num = outer_num + inner_num
    prior_den = outer_den + inner_den
    num_out = jnp.einsum(
        "thf,fhd->thd",
        phi_query,
        prior_num.reshape(PHI, heads, DV),
        precision=lax.Precision.HIGHEST,
    )
    den_out = jnp.einsum("thf,hf->th", phi_query, prior_den, precision=lax.Precision.HIGHEST)
    attended = (
        ((num_out + num_in) / (den_out + den_in)[..., None])
        .astype(jnp.bfloat16)
        .reshape(rows, heads * DV)
    )
    partial_out = jnp.dot(
        lax.all_gather(attended, "row", axis=0, tiled=True),
        out_weight,
        preferred_element_type=jnp.float32,
    ).astype(jnp.bfloat16)
    summed = lax.psum_scatter(
        partial_out.astype(jnp.float32).astype(jnp.bfloat16), "col", scatter_dimension=0, tiled=True
    )
    return summed


def solution(mesh):
    in_specs = (P(("ctx", "row"), "col"), P(None, "col"), P("col", "row"))
    out_specs = P(("ctx", "col"), "row")
    return jax.shard_map(shards, mesh=mesh, in_specs=in_specs, out_specs=out_specs, check_vma=False)
```

profile of v0, /device:TPU:16, one launch (start us, length us, event | category | flops | bytes accessed | tf_op | source)
XLA Modules:
  0.0 321.4 jit_solution(8538381725146888905)
XLA Ops:
  6.5 0.8 slice.31
  7.3 3.4 %collective-permute-start = (bf16[2,2176]{1,0:T(2,128)(2,1)S(1)}, bf16[2,2176]{1,0:T(2,128)(2,1)S(1)}, u32[]{:S(2)}, u32[]{:S(2)}) collective-permute-start(bf16[2,2176]{1,0:T(2,128)(2,1)S(1)} %slice.31), channel_id=1, source_target_pairs={{0,4},{4,8},{8,12},{12,16},{16,20},{20,24},{24,28},{28,32},{32,36}... | collective-permute-start | bytes 26120 | tf_op jit(solution)/shard_map/ppermute | solution.py:15
  10.7 0.9 slice_reduce_fusion.2
  11.7 0.7 pad_clamp_fusion.1
  12.4 0.7 pad_clamp_fusion
  13.0 0.0 collective-permute-done
  13.1 1.5 maximum_convert_fusion
  14.5 0.8 fusion.2
  15.3 0.7 copy.31
  16.1 0.9 gather_fusion
  17.0 0.9 gather_fusion.1
  18.0 0.0 copy-start.3
  18.0 0.9 gather_fusion.2
  18.9 0.9 gather_fusion.3
  19.9 0.4 fusion.11
  20.2 0.9 copy-done.1
  21.1 1.2 fusion.7
  22.4 0.5 copy.37
  22.9 1.2 convert_element_type.96
  24.1 0.0 all-gather.8.cloned.1.call-update
  24.1 40.8 %all-gather.8.cloned.1.call-done = bf16[4,153,2048]{2,1,0:T(8,128)(2,1)} async-done(((bf16[1,153,2048]{2,1,0:T(8,128)(2,1)}), bf16[4,153,2048]{2,1,0:T(8,128)(2,1)}) %all-gather.8.cloned.1.call-update) | async-done | bytes 2506768 | tf_op jit(solution)/shard_map/all_gather | solution.py:21
  64.9 0.7 all-reduce.2.cloned.1.call-update
  65.6 0.0 all-gather.6.cloned.1.call-start
  65.6 51.3 %all-reduce.2.cloned.1.call-done = bf16[1,153,2048]{2,1,0:T(8,128)(2,1)} async-done(((bf16[1,153,2048]{2,1,0:T(8,128)(2,1)}), bf16[1,153,2048]{2,1,0:T(8,128)(2,1)}) %all-reduce.2.cloned.1.call-update) | async-done | bytes 626704 | tf_op jit(solution)/shard_map/psum | solution.py:83
  116.9 0.0 all-gather.6.cloned.1.call-update
  116.9 0.0 all-gather.10.cloned.1.call-start
  117.0 0.3 fusion.15
  117.4 9.6 %psum.15 = bf16[1,4,153]{2,1,0:T(4,128)(2,1)S(1)} all-reduce(bf16[1,4,153]{2,1,0:T(4,128)(2,1)S(1)} %bitcast.43), channel_id=1, replica_groups=mesh['ctx'=16,'row'=4,'col'=4] {'row'}, use_global_device_ids=true, to_apply=%region_5.6 | all-reduce | flops 612 | bytes 2448 | tf_op jit(solution)/shard_map/psum | solution.py:84
  126.9 10.4 %all-gather.1 = bf16[4,4,153]{2,1,0:T(4,128)(2,1)S(1)} all-gather(bf16[1,4,153]{2,1,0:T(4,128)(2,1)S(1)} %bitcast.44), channel_id=2, replica_groups=mesh['ctx'=16,'row'=4,'col'=4] {'row'}, dimensions={0}, use_global_device_ids=true | all-gather | bytes 6120 | tf_op jit(solution)/shard_map/all_gather | solution.py:21
  137.3 17.5 %all_gather.20 = bf16[16,4,153]{2,1,0:T(4,128)(2,1)S(1)} all-gather(bf16[1,4,153]{2,1,0:T(4,128)(2,1)S(1)} %psum.15), channel_id=1, replica_groups=mesh['ctx'=16,'row'=4,'col'=4] {'ctx'}, dimensions={0}, use_global_device_ids=true | all-gather | bytes 20808 | tf_op jit(solution)/shard_map/all_gather | solution.py:92
  154.8 0.1 select_reduce_fusion.1
  154.9 2.1 convert_reduce_fusion
  157.0 0.1 broadcast_in_dim.68
  157.2 0.2 while.12
  157.4 0.5 fusion.14
  157.9 27.6 %all-gather.6.cloned.1.call-done = bf16[16,153,2048]{2,1,0:T(8,128)(2,1)} async-done(((bf16[1,153,2048]{2,1,0:T(8,128)(2,1)}), bf16[16,153,2048]{2,1,0:T(8,128)(2,1)}) %all-gather.6.cloned.1.call-update) | async-done | bytes 10027024 | tf_op jit(solution)/shard_map/all_gather | solution.py:89
  185.6 6.8 %select_reduce_fusion = f32[153,2048]{1,0:T(8,128)S(1)} fusion(bf16[16,153,2048]{2,1,0:T(8,128)(2,1)} %all-gather.6.cloned.1.call-done, pred[16]{0:T(512)(128)(4,1)S(1)} %iota_compare_fusion.1), kind=kLoop, calls=%fused_computation.6 | loop fusion | flops 14727168 | bytes 11280400 | tf_op jit(solution)/shard_map/reduce_sum | solution.py:97
  192.4 0.2 add.70
  192.6 0.8 reshape.56
  193.5 0.0 copy-start.4
  193.5 3.7 %fusion.5 = f32[4,512,256]{2,1,0:T(8,128)S(1)} fusion(f32[153,4,512]{2,1,0:T(4,128)S(1)} %reshape.56, f32[256,4,136]{0,2,1:T(8,128)S(1)} %get-tuple-element.60, f32[256,4,16]{0,2,1:T(8,128)S(1)} %get-tuple-element.56, f32[153]{0:T(256)S(1)} %pad.3.clone), kind=kOutput, calls=%fused_computation.17 | convolution fusion | flops 962906112 | bytes 3973732 | tf_op jit(solution)/shard_map/thf,fhd->thd/dot_general | solution.py:103
  197.2 1.4 fusion.4
  198.6 0.0 all-gather.10.cloned.1.call-update
  198.6 0.3 reduce-scatter.2.cloned.1.call-start
  198.9 52.9 %all-gather.10.cloned.1.call-done = bf16[1024,2048]{0,1:T(8,128)(2,1)} async-done(((bf16[256,2048]{0,1:T(8,128)(2,1)}), bf16[1024,2048]{0,1:T(8,128)(2,1)}) %all-gather.10.cloned.1.call-update) | async-done | bytes 4194320 | tf_op jit(solution)/shard_map/all_gather | solution.py:116
  251.8 14.0 %convolution_convert_fusion = bf16[1024,2048]{1,0:T(8,128)(2,1)} fusion(bf16[1024,2048]{0,1:T(8,128)(2,1)} %all-gather.10.cloned.1.call-done, bf16[2048,2048]{1,0:T(8,128)(2,1)} %param.17), kind=kOutput, calls=%fused_computation.7 | convolution fusion | flops 8592031744 | bytes 16777216 | tf_op jit(solution)/shard_map/dot_general | solution.py:115
  265.9 0.0 reduce-scatter.2.cloned.1.call-update
  265.9 49.0 %reduce-scatter.2.cloned.1.call-done = bf16[256,2048]{1,0:T(8,128)(2,1)} async-done(((bf16[1024,2048]{1,0:T(8,128)(2,1)}), bf16[256,2048]{1,0:T(8,128)(2,1)}) %reduce-scatter.2.cloned.1.call-update) | async-done | bytes 1048592 | tf_op jit(solution)/shard_map/reduce_scatter | solution.py:120
  (19 shorter events, 0.2 us)
Async XLA Ops:
  6.5 58.3 %all-gather.8.cloned.1.call-start = ((), (), s32[]{:S(2)}) async-start(), calls=%async_computation.3 | async-start | bytes 3276800 | tf_op jit(solution)/shard_map/all_gather | solution.py:21
  7.3 5.7 %collective-permute-start = (bf16[2,2176]{1,0:T(2,128)(2,1)S(1)}, bf16[2,2176]{1,0:T(2,128)(2,1)S(1)}, u32[]{:S(2)}, u32[]{:S(2)}) collective-permute-start(bf16[2,2176]{1,0:T(2,128)(2,1)S(1)} %slice.31), channel_id=1, source_target_pairs={{0,4},{4,8},{8,12},{12,16},{16,20},{20,24},{24,28},{28,32},{32,36}... | collective-permute-start | bytes 26120 | tf_op jit(solution)/shard_map/ppermute | solution.py:15
  16.0 3.8 %copy-start = (bf16[256,2176]{0,1:T(8,128)(2,1)}, bf16[256,2176]{0,1:T(8,128)(2,1)S(1)}, u32[]{:S(2)}) copy-start(bf16[256,2176]{0,1:T(8,128)(2,1)S(1)} %copy.31) | copy-start | bytes 3342340
  18.0 1.9 copy-start.3
  19.9 1.2 copy-start.1
  64.9 52.1 %all-reduce.2.cloned.1.call-start = ((), (), s32[]{:S(2)}) async-start(), calls=%async_computation.1 | async-start | bytes 1310720 | tf_op jit(solution)/shard_map/psum | solution.py:83
  65.6 120.0 %all-gather.6.cloned.1.call-start = ((), (), s32[]{:S(2)}) async-start(), calls=%async_computation.2 | async-start | bytes 11141120 | tf_op jit(solution)/shard_map/all_gather | solution.py:89
  116.9 134.9 %all-gather.10.cloned.1.call-start = ((), (), s32[]{:S(2)}) async-start(), calls=%async_computation.4 | async-start | bytes 5242880 | tf_op jit(solution)/shard_map/all_gather | solution.py:116
  193.4 3.7 %copy-start.2 = (bf16[256,2176]{0,1:T(8,128)(2,1)S(1)}, bf16[256,2176]{0,1:T(8,128)(2,1)}, u32[]{:S(2)}) copy-start(bf16[256,2176]{0,1:T(8,128)(2,1)} %copy-done) | copy-start | bytes 3342340
  193.5 3.7 %copy-start.4 = (bf16[4,256,256]{1,2,0:T(8,128)(2,1)S(1)}, bf16[4,256,256]{1,2,0:T(8,128)(2,1)}, u32[]{:S(2)}) copy-start(bf16[4,256,256]{1,2,0:T(8,128)(2,1)} %get-tuple-element.63) | copy-start | bytes 1572868
  198.6 116.2 %reduce-scatter.2.cloned.1.call-start = ((), (), s32[]{:S(2)}) async-start(), calls=%async_computation.5 | async-start | bytes 5242880 | tf_op jit(solution)/shard_map/reduce_scatter | solution.py:120
Sparse Core Ops, SparseCore 0:
  24.2 40.5 all-gather.7
  68.0 48.8 all-reduce.1
  118.8 66.7 all-gather.5
  198.7 53.0 all-gather.9
  266.0 48.7 reduce-scatter.1
where the time goes:
time: 325 us; the launch traced here: 321 us
  waiting for transfers between devices  222 us (68%)
  blocking collectives  37.5 us (12%)
  matrix products  23 us (7%)
  between operations  13.4 us (4%)
  other arithmetic  11.5 us (4%)
  local copies, waits for them, and re-layouts  9.74 us (3%)
  starting transfers between devices  3.74 us (1%)
    all_gather x1, waiting for transfers between devices, shards(): lax.all_gather(attended, 'row', axis=0, tiled=True)  52.9 us
    psum x1, waiting for transfers between devices, shards(): lax.psum(local_num.astype(jnp.bfloat16), 'row').astype(jnp.float32)  51.3 us
    reduce_scatter x1, waiting for transfers between devices, shards(): lax.psum_scatter(partial_out.astype(jnp.float32).astype(jnp.bfloat16), 'c...  49 us
    all_gather x1, waiting for transfers between devices, entering(): lax.all_gather(a.astype(kind), axis)  40.8 us
    all_gather x1, waiting for transfers between devices, shards(): lax.all_gather(group_num[None].astype(jnp.bfloat16), 'ctx', axis=0, tiled...  27.6 us
    all_gather x1, blocking collectives, shards(): lax.all_gather(group_den[None].astype(jnp.bfloat16), 'ctx', axis=0, tiled...  17.5 us
    dot_general x1, matrix products, shards(): jnp.dot(lax.all_gather(attended, 'row', axis=0, tiled=True), out_weight,...  14 us
    all_gather x1, blocking collectives, entering(): lax.all_gather(a.astype(kind), axis)  10.4 us
  transfers between devices with their start and end apart: 6, of which 5 were waited for; matrix products, arithmetic and copies ran while one was open for 2% of the time, Pallas kernels for 0%

commit v1 on v0

v1 whole, which is shorter than its diff:
```python
import jax
import jax.numpy as jnp
import numpy as np
from jax import lax
from jax.experimental import pallas as pl
from jax.experimental.pallas import tpu as pltpu
from jax.sharding import PartitionSpec as P

MESH = pl.DeviceIdType.MESH
FEAT = 16
DV = 512
PHI = 153
WIN = 640
BLK = 256
ROWS = 4
CTX = 16
TOK = ROWS * BLK
FP = 256
FS = 192
SR, SC = 48, 128
K = 8
T = BLK // K
CH = 4 * T
HALF = 1024
Q0, K0 = 96, 112
F32, BF16 = jnp.float32, jnp.bfloat16
NT = (((1,), (1,)), ((), ()))


def selectors():
    first, second = np.triu_indices(FEAT)
    k1, k2, q1, q2 = (np.zeros((128, FP), np.float32) for _ in range(4))
    for m in (k1, k2, q1, q2):
        m[0, 0] = 1.0
    for i in range(FEAT):
        k1[K0 + i, 1 + i] = 1.0
        k2[0, 1 + i] = 1.0
        q1[Q0 + i, 1 + i] = 1.0
        q2[0, 1 + i] = 0.25
    for n, (i, j) in enumerate(zip(first, second)):
        at = 1 + FEAT + n
        k1[K0 + i, at] = 1.0
        k2[K0 + j, at] = 1.0
        q1[Q0 + i, at] = 1.0
        q2[Q0 + j, at] = 1.0 / 32 if i == j else 1.0 / 16
    move = np.zeros((128, 128), np.float32)
    for i in range(FEAT):
        move[Q0 + i, K0 + i] = 0.25
    return k1.T, k2.T, q1, q2, move


def dot(a, b):
    return jnp.dot(a, b, preferred_element_type=F32)


def dot_nt(a, b):
    return lax.dot_general(a, b, NT, preferred_element_type=F32)


def kernel(
    proj, taps, weight, k1, k2, q1, q2, move, out,
    raw, gated, num, den, phiq, inner, mine, z1, z2, outer, w, att, part, own, opp, left_in, right_in,
    xs, xr, ts, tr, ws, z1s, z1r, z2s, z2r, ags, agr, rss, rsr,
):
    c, h, g = lax.axis_index("ctx"), lax.axis_index("row"), lax.axis_index("col")

    def at(axis, index, by, n):
        return {axis: lax.rem(index + by, n)}

    def row(by):
        return at("row", h, by, ROWS)

    def ctx(by):
        return at("ctx", c, by, CTX)

    right, left = at("col", g, 1, 4), at("col", g, 3, 4)
    sends_tail = jnp.logical_and(h == ROWS - 1, c < CTX - 1)

    load_w = pltpu.make_async_copy(weight, w, ws)
    load_w.start()

    bar = pltpu.get_barrier_semaphore()

    def greet(where):
        pl.semaphore_signal(bar, inc=1, device_id=where, device_id_type=MESH)

    for i in range(1, ROWS):
        greet(row(i))

    @pl.loop(1, CTX)
    def _(i):
        greet(ctx(i))

    greet(right)
    greet(left)

    @pl.when(jnp.logical_and(h != ROWS - 1, c > 0))
    def _():
        greet({"ctx": c - 1, "row": ROWS - 1})

    pl.semaphore_wait(bar, ROWS - 1 + CTX - 1 + 2 + jnp.where(sends_tail, ROWS - 1, 0))

    def window(head):
        return pl.ds(pl.multiple_of(head * DV, DV), WIN)

    def exchange(i):
        return pltpu.make_async_remote_copy(
            proj.at[:, window(lax.rem(h + i, ROWS))],
            raw.at[pl.ds(pl.multiple_of(16 + h * BLK, 16), BLK)],
            xs.at[i],
            xr.at[i],
            row(i),
            MESH,
        )

    def tail(head):
        return pltpu.make_async_remote_copy(
            proj.at[pl.ds(BLK - 16, 16), pl.ds(head * DV, WIN)],
            raw.at[pl.ds(0, 16)],
            ts.at[head],
            tr,
            {"ctx": lax.rem(c + 1, CTX), "row": head},
            MESH,
        )

    for i in (2, 1, 3):
        exchange(i).start()

    @pl.when(sends_tail)
    def _():
        for head in range(ROWS):
            tail(head).start()

    keep = pltpu.make_async_copy(
        proj.at[:, window(h)], raw.at[pl.ds(pl.multiple_of(16 + h * BLK, 16), BLK)], xs.at[0]
    )
    keep.start()
    keep.wait()

    @pl.when(c == 0)
    def _():
        raw[pl.ds(0, 16), :] = jnp.zeros((16, WIN), BF16)

    @pl.when(c > 0)
    def _():
        tail(0).wait_recv()

    for i in (1, 3, 2):
        exchange(i).wait_recv()

    tap = taps[:, window(h)]
    lane = lax.broadcasted_iota(jnp.int32, (BLK, 128), 1)
    feature = lax.broadcasted_iota(jnp.int32, (FS, DV), 0)
    ones = jnp.ones((8, BLK), BF16)
    inner[...] = jnp.zeros((FS, DV), F32)

    @pl.loop(0, ROWS)
    def _(b):
        x = raw[pl.ds(pl.multiple_of(b * BLK, 16), BLK + 16), :].astype(F32)
        y = x * (tap[0:1] * x + tap[1:2] * pltpu.roll(x, 1, 0) + tap[2:3] * pltpu.roll(x, 2, 0))
        y = pltpu.roll(y[16:], WIN - 2 * FEAT * (h + 1), 1)
        rows = pl.ds(pl.multiple_of(b * BLK, BLK), BLK)
        value = y[:, :DV].astype(BF16)
        qk = jnp.where(lane == 0, 1.0, y[:, DV:]).astype(BF16)
        gated[rows, :DV] = value
        gated[rows, DV:] = qk
        phik = (dot_nt(k1[...], qk) * dot_nt(k2[...], qk)).astype(BF16)
        total = dot_nt(ones, phik)[0:1]
        total = jnp.concatenate([total, jnp.zeros((1, DV - FP), F32)], axis=1)
        state = jnp.where(feature == PHI, total, dot(phik[:FS], value))
        before = inner[...]
        mine[b] = before.astype(BF16)
        inner[...] = before + state

    mine[ROWS] = inner[...].astype(BF16)

    def share(index):
        return (
            pl.ds(pl.multiple_of(lax.div(index, 4) * SR, SR), SR),
            pl.ds(pl.multiple_of(lax.rem(index, 4) * SC, SC), SC),
        )

    def to_owner(i):
        r, s = share(lax.rem(c + i, CTX))
        return pltpu.make_async_remote_copy(
            mine.at[ROWS, r, s], z1.at[c], z1s.at[i], z1r.at[i], ctx(i), MESH
        )

    def from_owner(i):
        r, s = share(c)
        return pltpu.make_async_remote_copy(
            z2.at[lax.rem(c + i, CTX)], outer.at[r, s], z2s.at[i], z2r.at[i], ctx(i), MESH
        )

    @pl.loop(1, CTX)
    def _(i):
        to_owner(i).start()

    r, s = share(c)
    z1[c] = mine[ROWS, r, s]
    outer[FS:, :] = jnp.zeros((FP - FS, DV), BF16)

    causal = lax.broadcasted_iota(jnp.int32, (BLK, BLK), 0) >= lax.broadcasted_iota(
        jnp.int32, (BLK, BLK), 1
    )

    @pl.loop(0, ROWS)
    def _(b):
        rows = pl.ds(pl.multiple_of(b * BLK, BLK), BLK)
        qk = gated[rows, DV:]
        value = gated[rows, :DV]
        phi = (dot(qk, q1[...]) * dot(qk, q2[...])).astype(BF16)
        phiq[rows, :] = phi
        z = dot_nt(dot(qk, move[...]).astype(BF16), qk)
        kern = jnp.where(causal, 1.0 + z + 0.5 * z * z, 0.0).astype(BF16)
        prior = mine[b]
        prior_total = prior[PHI : PHI + 1, :FP].astype(F32)
        num[rows, :] = dot(kern, value) + dot(phi[:, :FS], prior)
        weight_sum = jnp.sum(kern.astype(F32), axis=1, keepdims=True) + jnp.sum(
            phi.astype(F32) * prior_total, axis=1, keepdims=True
        )
        den[rows, :] = jnp.broadcast_to(weight_sum, (BLK, 128))

    @pl.loop(1, CTX)
    def _(i):
        to_owner(i).wait_recv()

    run = jnp.zeros((SR, SC), F32)
    for i in range(CTX):
        z2[i] = run.astype(BF16)
        run = run + z1[i].astype(F32)

    @pl.loop(1, CTX)
    def _(i):
        from_owner(i).start()

    r, s = share(c)
    outer[r, s] = z2[c]

    @pl.loop(1, CTX)
    def _(i):
        from_owner(i).wait_recv()

    load_w.wait()

    def head(by):
        return pl.ds(pl.multiple_of(lax.rem(h + by, ROWS) * DV, DV), DV)

    def ag(k, which):
        rows, of, to = (
            (pl.ds(0, CH), 0, 1),
            (pl.ds(0, CH), 0, 3),
            (pl.ds(0, CH // 2), 3, 1),
            (pl.ds(CH // 2, CH // 2), 1, 3),
        )[which]
        return pltpu.make_async_remote_copy(
            att.at[k, rows, head(of)],
            att.at[k, rows, head(of)],
            ags.at[k, which],
            agr.at[k, which],
            row(to),
            MESH,
        )

    def rs(k, which):
        a, b = pl.ds(0, HALF), pl.ds(HALF, HALF)
        j, cols, land, to = (
            (2, a, opp.at[k, 0], right),
            (2, b, opp.at[k, 1], left),
            (1, b, left_in.at[k, :, b], right),
            (3, a, right_in.at[k, :, a], left),
            (1, a, left_in.at[k, :, a], right),
            (3, b, right_in.at[k, :, b], left),
        )[which]
        return pltpu.make_async_remote_copy(
            part.at[k, pl.ds(j * T, T), cols], land, rss.at[k, which], rsr.at[k, which], to, MESH
        )

    outer_total = outer[PHI : PHI + 1, :FP].astype(F32)

    @pl.loop(0, K + 4)
    def _(step):
        @pl.when(step < K)
        def _():
            k = step
            spots = [
                pl.ds(pl.multiple_of(lax.rem(g + j, ROWS) * BLK + k * T, T), T) for j in range(4)
            ]
            phi = jnp.concatenate([phiq[spot, :] for spot in spots], axis=0)
            top = jnp.concatenate([num[spot, :] for spot in spots], axis=0) + dot(phi, outer[...])
            bottom = jnp.concatenate([den[spot, :] for spot in spots], axis=0)[:, 0:1] + jnp.sum(
                phi.astype(F32) * outer_total, axis=1, keepdims=True
            )
            att[k, :, head(0)] = (top / bottom).astype(BF16)
            ag(k, 0).start()
            ag(k, 1).start()

        @pl.when(jnp.logical_and(step >= 1, step < K + 1))
        def _():
            k = step - 1
            ag(k, 0).wait_recv()
            ag(k, 2).start()
            ag(k, 1).wait_recv()
            ag(k, 3).start()

        @pl.when(jnp.logical_and(step >= 2, step < K + 2))
        def _():
            k = step - 2
            ag(k, 2).wait_recv()
            ag(k, 3).wait_recv()
            for half in range(2):
                for n in range(2):
                    cols = slice(half * HALF + n * 512, half * HALF + n * 512 + 512)
                    p = dot(att[k], w[:, cols])
                    own[k, :, cols] = p[:T]
                    part[k, T:, cols] = p[T:].astype(BF16)
                for which in ((0, 3), (1, 2))[half]:
                    rs(k, which).start()

        @pl.when(jnp.logical_and(step >= 3, step < K + 3))
        def _():
            k = step - 3
            rs(k, 0).wait_recv()
            part[k, T : 2 * T, :HALF] = (
                part[k, T : 2 * T, :HALF].astype(F32) + opp[k, 0].astype(F32)
            ).astype(BF16)
            rs(k, 4).start()
            rs(k, 1).wait_recv()
            part[k, 3 * T :, HALF:] = (
                part[k, 3 * T :, HALF:].astype(F32) + opp[k, 1].astype(F32)
            ).astype(BF16)
            rs(k, 5).start()

        @pl.when(step >= 4)
        def _():
            k = step - 4
            for which in range(2, 6):
                rs(k, which).wait_recv()
            out[pl.ds(pl.multiple_of(k * T, T), T), :] = (
                own[k] + left_in[k].astype(F32) + right_in[k].astype(F32)
            ).astype(BF16)

    for i in (1, 2, 3):
        exchange(i).wait_send()

    @pl.when(sends_tail)
    def _():
        for one in range(ROWS):
            tail(one).wait_send()

    @pl.loop(1, CTX)
    def _(i):
        to_owner(i).wait_send()
        from_owner(i).wait_send()

    @pl.loop(0, K)
    def _(k):
        for which in range(4):
            ag(k, which).wait_send()
        for which in range(6):
            rs(k, which).wait_send()


def shards(projected, conv_taps, out_weight):
    constants = [jnp.asarray(m, BF16) for m in selectors()]
    vmem = pl.BlockSpec(memory_space=pltpu.VMEM)
    hbm = pl.BlockSpec(memory_space=pl.ANY)
    dma = pltpu.SemaphoreType.DMA
    return pl.pallas_call(
        kernel,
        out_shape=jax.ShapeDtypeStruct((BLK, 2048), BF16),
        in_specs=[hbm, vmem, hbm] + [vmem] * 5,
        out_specs=vmem,
        scratch_shapes=[
            pltpu.VMEM((16 + TOK, WIN), BF16),
            pltpu.VMEM((TOK, WIN), BF16),
            pltpu.VMEM((TOK, DV), F32),
            pltpu.VMEM((TOK, 128), F32),
            pltpu.VMEM((TOK, FP), BF16),
            pltpu.VMEM((FS, DV), F32),
            pltpu.VMEM((ROWS + 1, FS, DV), BF16),
            pltpu.VMEM((CTX, SR, SC), BF16),
            pltpu.VMEM((CTX, SR, SC), BF16),
            pltpu.VMEM((FP, DV), BF16),
            pltpu.VMEM((2048, 2048), BF16),
            pltpu.VMEM((K, CH, 2048), BF16),
            pltpu.VMEM((K, CH, 2048), BF16),
            pltpu.VMEM((K, T, 2048), F32),
            pltpu.VMEM((K, 2, T, HALF), BF16),
            pltpu.VMEM((K, T, 2048), BF16),
            pltpu.VMEM((K, T, 2048), BF16),
            dma((4,)),
            dma((4,)),
            dma((4,)),
            dma,
            dma,
            dma((CTX,)),
            dma((CTX,)),
            dma((CTX,)),
            dma((CTX,)),
            dma((K, 4)),
            dma((K, 4)),
            dma((K, 6)),
            dma((K, 6)),
        ],
        compiler_params=pltpu.CompilerParams(
            collective_id=0, has_side_effects=True, vmem_limit_bytes=56 * 2**20
        ),
    )(projected, conv_taps, out_weight, *constants)


def solution(mesh):
    in_specs = (P(("ctx", "row"), "col"), P(None, "col"), P("col", "row"))
    out_specs = P(("ctx", "col"), "row")
    return jax.shard_map(shards, mesh=mesh, in_specs=in_specs, out_specs=out_specs, check_vma=False)
```

time: 325 us -> 100 us (0.31)
  waiting for transfers between devices: 222 us -> 0 us
  Pallas kernels: 0 us -> 96.8 us
  blocking collectives: 37.5 us -> 0 us
  matrix products: 23 us -> 0 us
  between operations: 13.4 us -> 0.01 us
  other arithmetic: 11.5 us -> 0 us
  local copies, waits for them, and re-layouts: 9.74 us -> 2.3 us
  starting transfers between devices: 3.74 us -> 0 us
    all_gather x3 -> x0, waiting for transfers between devices: 121 us -> none  [the longest x1 52.9 us: shards(): lax.all_gather(attended, 'row', axis=0, tiled=True)]
    pallas_call x0 -> x1, Pallas kernels: none -> 96.8 us  [shards(): pl.pallas_call(kernel, out_shape=jax.ShapeDtypeStruct((BLK, 2048), BF16),...]
    psum x1 -> x0, waiting for transfers between devices: 51.3 us -> none  [shards(): lax.psum(local_num.astype(jnp.bfloat16), 'row').astype(jnp.float32)]
    reduce_scatter x1 -> x0, waiting for transfers between devices: 49 us -> none  [shards(): lax.psum_scatter(partial_out.astype(jnp.float32).astype(jnp.bfloat16), 'c...]
    all_gather x2 -> x0, blocking collectives: 27.9 us -> none  [the longest x1 17.5 us: shards(): lax.all_gather(group_den[None].astype(jnp.bfloat16), 'ctx', axis=0, tiled...]
    dot_general x6 -> x0, matrix products: 23 us -> none  [the longest x1 14 us: shards(): jnp.dot(lax.all_gather(attended, 'row', axis=0, tiled=True), out_weight,...]
    psum x1 -> x0, blocking collectives: 9.57 us -> none  [shards(): lax.psum(local_den.astype(jnp.bfloat16), 'row').astype(jnp.float32)]
    reduce_sum x3 -> x0, other arithmetic: 7.23 us -> none  [the longest x1 6.82 us: shards(): summed_num = jnp.sum(jnp.where(keep[:, None, None], pieces[0], 0.0), axis=0)]
  transfers between devices with their start and end apart: 6 -> 0, of which waited for: 5 -> 0; matrix products, arithmetic and copies ran while one was open for 2% -> 0% of each run, Pallas kernels for 0% -> 0%
where the time goes in v1:
time: 100 us; the launch traced here: 99.1 us
  Pallas kernels  96.8 us (97%)
  local copies, waits for them, and re-layouts  2.3 us (2%)
    pallas_call x1, Pallas kernels, shards(): pl.pallas_call(kernel, out_shape=jax.ShapeDtypeStruct((BLK, 2048), BF16),...  96.8 us
    unnamed x1, local copies, waits for them, and re-layouts  2.3 us

profile of v1, /device:TPU:16, one launch (start us, length us, event | category | flops | bytes accessed | tf_op | source)
XLA Modules:
  0.0 99.1 jit_solution(346146198297381986)
XLA Ops:
  0.0 96.8 %shard_map.82 = bf16[256,2048]{1,0:T(8,128)(2,1)} custom-call(bf16[256,2176]{1,0:T(8,128)(2,1)} %proj.1, f32[3,2176]{1,0:T(4,128)} %taps.1, bf16[2048,2048]{1,0:T(8,128)(2,1)} %weight.1, bf16[256,128]{1,0:T(8,128)(2,1)} %constant.10.clone.k1, bf16[256,128]{1,0:T(8,128)(2,1)} %constant.11.clone.k2, bf16[128,256]{1,0:T(8,128)(2,1)} %constant.12.clone.q1, ...), custom_call_target="tpu_custom_call" | custom-call | tf_op jit(solution)/shard_map/pallas_call | solution.py:369
  96.8 2.3 %copy.10 = bf16[256,2048]{1,0:T(8,128)(2,1)} copy(bf16[256,2048]{1,0:T(8,128)(2,1)} %shard_map.82) | data formatting | bytes 2097152

commit v2 on v1

v2 whole, which is shorter than its diff:
```python
import jax
import jax.numpy as jnp
import numpy as np
from jax import lax
from jax.experimental import pallas as pl
from jax.experimental.pallas import tpu as pltpu
from jax.sharding import PartitionSpec as P

MESH = pl.DeviceIdType.MESH
FEAT = 16
DV = 512
PHI = 153
WIN = 640
BLK = 256
ROWS = 4
CTX = 16
TOK = ROWS * BLK
FP = 256
FS = 192
SR, SC = 48, 128
TILES = 5
K = 8
T = BLK // K
CH = 4 * T
HALF = 1024
Q0, K0 = 96, 112
F32, BF16 = jnp.float32, jnp.bfloat16
NT = (((1,), (1,)), ((), ()))


def selectors():
    first, second = np.triu_indices(FEAT)
    k1, k2, q1, q2 = (np.zeros((FP, 128), np.float32) for _ in range(4))
    for m in (k1, k2, q1, q2):
        m[0, 0] = 1.0
    for i in range(FEAT):
        k1[1 + i, K0 + i] = 1.0
        k2[1 + i, 0] = 1.0
        q1[1 + i, Q0 + i] = 1.0
        q2[1 + i, 0] = 0.25
    for n, (i, j) in enumerate(zip(first, second)):
        at = 1 + FEAT + n
        k1[at, K0 + i] = 1.0
        k2[at, K0 + j] = 1.0
        q1[at, Q0 + i] = 1.0
        q2[at, Q0 + j] = 1.0 / 32 if i == j else 1.0 / 16
    move = np.zeros((128, 128), np.float32)
    for i in range(FEAT):
        move[K0 + i, Q0 + i] = 0.25
    return np.concatenate([k1, k2, q1, q2, move])


def dot(a, b):
    return jnp.dot(a, b, preferred_element_type=F32)


def dot_nt(a, b):
    return lax.dot_general(a, b, NT, preferred_element_type=F32)


def kernel(
    proj, taps, weight, select, out,
    x, packed, quarter, raw, land, tap, gated, phik, totals, num, den, phiq,
    inner, mine, z1, z2, outer, w, att, part, own, opp, left_in, right_in,
    ps, xs, xr, ts, tr, ws, z1s, z1r, z2s, z2r, ags, agr, rss, rsr,
):
    c, h, g = lax.axis_index("ctx"), lax.axis_index("row"), lax.axis_index("col")

    def at(axis, index, by, n):
        return {axis: lax.rem(index + by, n)}

    def row(by):
        return at("row", h, by, ROWS)

    right, left = at("col", g, 1, 4), at("col", g, 3, 4)
    sends_tail = jnp.logical_and(h == ROWS - 1, c < CTX - 1)

    load_x = pltpu.make_async_copy(proj, x, ps)
    load_x.start()
    load_w = pltpu.make_async_copy(weight, w, ws)
    load_w.start()

    bar = pltpu.get_barrier_semaphore()

    def greet(where):
        pl.semaphore_signal(bar, inc=1, device_id=where, device_id_type=MESH)

    @pl.loop(1, CTX)
    def _(i):
        greet(at("ctx", c, i, CTX))

    @pl.when(jnp.logical_and(h != ROWS - 1, c > 0))
    def _():
        greet({"ctx": c - 1, "row": ROWS - 1})

    for i in range(1, ROWS):
        greet(row(i))
    greet(right)
    greet(left)

    lane = lax.broadcasted_iota(jnp.int32, (BLK, 128), 1)
    lane_q = lax.broadcasted_iota(jnp.int32, (BLK // 4, 128), 1)
    load_x.wait()
    for head in range(ROWS):
        y = pltpu.roll(
            x[:, head * DV : head * DV + WIN].astype(F32), WIN - 2 * FEAT * (head + 1), 1
        )
        for j in range(TILES):
            packed[head, j] = y[:, j * 128 : j * 128 + 128].astype(BF16)
        last = y[:, DV:]
        q = jnp.zeros((BLK // 4, 128), F32)
        for i in range(4):
            part_i = pltpu.roll(last[i * 64 : i * 64 + 64], 32 * (i + 1) % 128, 1)
            q = jnp.where(lane_q // 32 == i, part_i, q)
        quarter[head] = q.astype(BF16)
    window = taps[:, pl.ds(pl.multiple_of(h * DV, DV), WIN)]
    window = jnp.concatenate([window, jnp.zeros((5, WIN), F32)], axis=0)
    tap[...] = pltpu.roll(window, WIN - 2 * FEAT * (h + 1), 1)

    pl.semaphore_wait(bar, ROWS - 1 + CTX - 1 + 2 + jnp.where(sends_tail, ROWS - 1, 0))

    def spot(r):
        return pl.ds(pl.multiple_of(16 + r * BLK, 16), BLK)

    def send_values(i, j):
        return pltpu.make_async_remote_copy(
            packed.at[lax.rem(h + i, ROWS), j], raw.at[j, spot(h)], xs.at[i, j], xr.at[i, j], row(i), MESH
        )

    def send_keys(i):
        return pltpu.make_async_remote_copy(
            quarter.at[lax.rem(h + i, ROWS)], land.at[h], xs.at[i, 4], xr.at[i, 4], row(i), MESH
        )

    def tail(head):
        return pltpu.make_async_remote_copy(
            packed.at[head, :, pl.ds(BLK - 16, 16)],
            raw.at[:, pl.ds(0, 16)],
            ts.at[head],
            tr,
            {"ctx": lax.rem(c + 1, CTX), "row": head},
            MESH,
        )

    for i in (2, 1, 3):
        send_keys(i).start()

    @pl.when(sends_tail)
    def _():
        for head in range(ROWS):
            tail(head).start()

    for j in range(4):
        for i in (2, 1, 3):
            send_values(i, j).start()

    for j in range(4):
        raw[j, spot(h), :] = packed[h, j]
    land[h] = quarter[h]

    for i in (1, 3, 2):
        send_keys(i).wait_recv()
    for r in range(ROWS):
        q = land[r].astype(F32)
        for i in range(4):
            raw[4, 16 + r * BLK + i * 64 : 16 + r * BLK + i * 64 + 64, :] = pltpu.roll(
                q, 96 - 32 * i, 1
            ).astype(BF16)

    @pl.when(c == 0)
    def _():
        raw[:, 0:16, :] = jnp.zeros((TILES, 16, 128), BF16)

    @pl.when(c > 0)
    def _():
        tail(0).wait_recv()

    def gate(j, b, cols):
        v = raw[j, pl.ds(pl.multiple_of(b * BLK, 16), BLK + 16), :].astype(F32)
        t = [tap[i : i + 1, cols] for i in range(3)]
        return (v * (t[0] * v + t[1] * pltpu.roll(v, 1, 0) + t[2] * pltpu.roll(v, 2, 0)))[16:]

    ones = jnp.ones((8, BLK), BF16)
    k1, k2, q1, q2 = (select[i * FP : i * FP + FP] for i in range(4))
    move = select[4 * FP :]

    @pl.loop(0, ROWS)
    def _(b):
        qk = jnp.where(lane == 0, 1.0, gate(4, b, slice(DV, WIN))).astype(BF16)
        gated[pl.ds(pl.multiple_of(b * BLK, BLK), BLK), DV:] = qk
        phi = (dot_nt(k1, qk) * dot_nt(k2, qk)).astype(BF16)
        phik[b] = phi
        totals[b] = jnp.concatenate([dot_nt(ones, phi), jnp.zeros((8, DV - FP), F32)], axis=1)

    feature = lax.broadcasted_iota(jnp.int32, (FS, 128), 0)
    mine_rows = pl.ds(pl.multiple_of(lax.rem(c, 4) * SR, SR), SR)
    mine_cols = pl.ds(pl.multiple_of(lax.div(c, 4) * SC, SC), SC)

    def to_owner(o, source):
        return pltpu.make_async_remote_copy(
            mine.at[
                ROWS,
                pl.ds(pl.multiple_of(lax.rem(o, 4) * SR, SR), SR),
                pl.ds(pl.multiple_of(lax.div(o, 4) * SC, SC), SC),
            ],
            z1.at[source],
            z1s.at[o],
            z1r.at[source],
            {"ctx": o},
            MESH,
        )

    def from_owner(to, owner):
        return pltpu.make_async_remote_copy(
            z2.at[to], outer.at[mine_rows, mine_cols], z2s.at[to], z2r.at[owner], {"ctx": to}, MESH
        )

    def other(i):
        return lax.rem(c + i, CTX)

    def own_share():
        @pl.loop(1, CTX)
        def _(i):
            to_owner(c, other(i)).wait_recv()

        run = jnp.zeros((SR, SC), F32)
        for i in range(CTX):
            z2[i] = run.astype(BF16)
            run = run + z1[i].astype(F32)

        @pl.loop(1, CTX)
        def _(i):
            from_owner(other(i), c).start()

        outer[mine_rows, mine_cols] = z2[c]

    outer[FS:, :] = jnp.zeros((FP - FS, DV), BF16)

    @pl.loop(0, 4)
    def _(j):
        cols = pl.ds(pl.multiple_of(j * 128, 128), 128)
        for i in (1, 3, 2):
            send_values(i, j).wait_recv()
        inner[...] = jnp.zeros((FS, 128), F32)

        @pl.loop(0, ROWS)
        def _(b):
            value = gate(j, b, cols).astype(BF16)
            gated[pl.ds(pl.multiple_of(b * BLK, BLK), BLK), cols] = value
            state = jnp.where(
                feature == PHI, totals[b, 0:1, cols], dot(phik[b, :FS], value)
            )
            before = inner[...]
            mine[b, :, cols] = before.astype(BF16)
            inner[...] = before + state

        mine[ROWS, :, cols] = inner[...].astype(BF16)
        for i in range(4):
            o = j * 4 + i

            @pl.when(o != c)
            def _():
                to_owner(o, c).start()

            @pl.when(o == c)
            def _():
                z1[c] = mine[ROWS, mine_rows, mine_cols]

        @pl.when(lax.div(c, 4) == j - 1)
        def _():
            own_share()

    causal = lax.broadcasted_iota(jnp.int32, (BLK, BLK), 0) >= lax.broadcasted_iota(
        jnp.int32, (BLK, BLK), 1
    )

    @pl.loop(0, ROWS)
    def _(b):
        @pl.when(jnp.logical_and(b == 2, lax.div(c, 4) == 3))
        def _():
            own_share()

        rows = pl.ds(pl.multiple_of(b * BLK, BLK), BLK)
        qk = gated[rows, DV:]
        value = gated[rows, :DV]
        phi = (dot_nt(qk, q1) * dot_nt(qk, q2)).astype(BF16)
        phiq[rows, :] = phi
        z = dot_nt(dot_nt(qk, move).astype(BF16), qk)
        kern = jnp.where(causal, 1.0 + z + 0.5 * z * z, 0.0).astype(BF16)
        prior = mine[b]
        prior_total = prior[PHI : PHI + 1, :FP].astype(F32)
        num[rows, :] = dot(kern, value) + dot(phi[:, :FS], prior)
        weight_sum = jnp.sum(kern.astype(F32), axis=1, keepdims=True) + jnp.sum(
            phi.astype(F32) * prior_total, axis=1, keepdims=True
        )
        den[rows, :] = jnp.broadcast_to(weight_sum, (BLK, 128))

    @pl.loop(1, CTX)
    def _(i):
        from_owner(c, other(i)).wait_recv()

    load_w.wait()

    def head(by):
        return pl.ds(pl.multiple_of(lax.rem(h + by, ROWS) * DV, DV), DV)

    def ag(k, which):
        rows, of, to = (
            (pl.ds(0, CH), 0, 1),
            (pl.ds(0, CH), 0, 3),
            (pl.ds(0, CH // 2), 3, 1),
            (pl.ds(CH // 2, CH // 2), 1, 3),
        )[which]
        return pltpu.make_async_remote_copy(
            att.at[k, rows, head(of)],
            att.at[k, rows, head(of)],
            ags.at[k, which],
            agr.at[k, which],
            row(to),
            MESH,
        )

    def rs(k, which):
        a, b = pl.ds(0, HALF), pl.ds(HALF, HALF)
        j, cols, land, to = (
            (2, a, opp.at[k, 0], right),
            (2, b, opp.at[k, 1], left),
            (1, b, left_in.at[k, :, b], right),
            (3, a, right_in.at[k, :, a], left),
            (1, a, left_in.at[k, :, a], right),
            (3, b, right_in.at[k, :, b], left),
        )[which]
        return pltpu.make_async_remote_copy(
            part.at[k, pl.ds(j * T, T), cols], land, rss.at[k, which], rsr.at[k, which], to, MESH
        )

    outer_total = outer[PHI : PHI + 1, :FP].astype(F32)

    @pl.loop(0, K + 4)
    def _(step):
        @pl.when(step < K)
        def _():
            k = step
            places = [
                pl.ds(pl.multiple_of(lax.rem(g + j, ROWS) * BLK + k * T, T), T) for j in range(4)
            ]
            phi = jnp.concatenate([phiq[place, :] for place in places], axis=0)
            top = jnp.concatenate([num[place, :] for place in places], axis=0) + dot(phi, outer[...])
            bottom = jnp.concatenate([den[place, :] for place in places], axis=0)[:, 0:1] + jnp.sum(
                phi.astype(F32) * outer_total, axis=1, keepdims=True
            )
            att[k, :, head(0)] = (top / bottom).astype(BF16)
            ag(k, 0).start()
            ag(k, 1).start()

        @pl.when(jnp.logical_and(step >= 1, step < K + 1))
        def _():
            k = step - 1
            ag(k, 0).wait_recv()
            ag(k, 2).start()
            ag(k, 1).wait_recv()
            ag(k, 3).start()

        @pl.when(jnp.logical_and(step >= 2, step < K + 2))
        def _():
            k = step - 2
            ag(k, 2).wait_recv()
            ag(k, 3).wait_recv()
            for half in range(2):
                for n in range(2):
                    cols = slice(half * HALF + n * 512, half * HALF + n * 512 + 512)
                    p = dot(att[k], w[:, cols])
                    own[k, :, cols] = p[:T]
                    part[k, T:, cols] = p[T:].astype(BF16)
                for which in ((0, 3), (1, 2))[half]:
                    rs(k, which).start()

        @pl.when(jnp.logical_and(step >= 3, step < K + 3))
        def _():
            k = step - 3
            rs(k, 0).wait_recv()
            part[k, T : 2 * T, :HALF] = (
                part[k, T : 2 * T, :HALF].astype(F32) + opp[k, 0].astype(F32)
            ).astype(BF16)
            rs(k, 4).start()
            rs(k, 1).wait_recv()
            part[k, 3 * T :, HALF:] = (
                part[k, 3 * T :, HALF:].astype(F32) + opp[k, 1].astype(F32)
            ).astype(BF16)
            rs(k, 5).start()

        @pl.when(step >= 4)
        def _():
            k = step - 4
            for which in range(2, 6):
                rs(k, which).wait_recv()
            out[pl.ds(pl.multiple_of(k * T, T), T), :] = (
                own[k] + left_in[k].astype(F32) + right_in[k].astype(F32)
            ).astype(BF16)

    for i in (1, 2, 3):
        send_keys(i).wait_send()
        for j in range(4):
            send_values(i, j).wait_send()

    @pl.when(sends_tail)
    def _():
        for one in range(ROWS):
            tail(one).wait_send()

    @pl.loop(1, CTX)
    def _(i):
        to_owner(other(i), c).wait_send()
        from_owner(other(i), c).wait_send()

    @pl.loop(0, K)
    def _(k):
        for which in range(4):
            ag(k, which).wait_send()
        for which in range(6):
            rs(k, which).wait_send()


def shards(projected, conv_taps, out_weight):
    select = jnp.asarray(selectors(), BF16)
    vmem = pl.BlockSpec(memory_space=pltpu.VMEM)
    hbm = pl.BlockSpec(memory_space=pl.ANY)
    dma = pltpu.SemaphoreType.DMA
    return pl.pallas_call(
        kernel,
        out_shape=jax.ShapeDtypeStruct((BLK, 2048), BF16),
        in_specs=[hbm, vmem, hbm, vmem],
        out_specs=vmem,
        scratch_shapes=[
            pltpu.VMEM((BLK, ROWS * (2 * FEAT + DV)), BF16),
            pltpu.VMEM((ROWS, TILES, BLK, 128), BF16),
            pltpu.VMEM((ROWS, BLK // 4, 128), BF16),
            pltpu.VMEM((TILES, 16 + TOK, 128), BF16),
            pltpu.VMEM((ROWS, BLK // 4, 128), BF16),
            pltpu.VMEM((8, WIN), F32),
            pltpu.VMEM((TOK, WIN), BF16),
            pltpu.VMEM((ROWS, FP, BLK), BF16),
            pltpu.VMEM((ROWS, 8, DV), F32),
            pltpu.VMEM((TOK, DV), F32),
            pltpu.VMEM((TOK, 128), F32),
            pltpu.VMEM((TOK, FP), BF16),
            pltpu.VMEM((FS, 128), F32),
            pltpu.VMEM((ROWS + 1, FS, DV), BF16),
            pltpu.VMEM((CTX, SR, SC), BF16),
            pltpu.VMEM((CTX, SR, SC), BF16),
            pltpu.VMEM((FP, DV), BF16),
            pltpu.VMEM((2048, 2048), BF16),
            pltpu.VMEM((K, CH, 2048), BF16),
            pltpu.VMEM((K, CH, 2048), BF16),
            pltpu.VMEM((K, T, 2048), F32),
            pltpu.VMEM((K, 2, T, HALF), BF16),
            pltpu.VMEM((K, T, 2048), BF16),
            pltpu.VMEM((K, T, 2048), BF16),
            dma,
            dma((4, TILES)),
            dma((4, TILES)),
            dma((4,)),
            dma,
            dma,
            dma((CTX,)),
            dma((CTX,)),
            dma((CTX,)),
            dma((CTX,)),
            dma((K, 4)),
            dma((K, 4)),
            dma((K, 6)),
            dma((K, 6)),
        ],
        compiler_params=pltpu.CompilerParams(
            collective_id=0, has_side_effects=True, vmem_limit_bytes=56 * 2**20
        ),
    )(projected, conv_taps, out_weight, select)


def solution(mesh):
    in_specs = (P(("ctx", "row"), "col"), P(None, "col"), P("col", "row"))
    out_specs = P(("ctx", "col"), "row")
    return jax.shard_map(shards, mesh=mesh, in_specs=in_specs, out_specs=out_specs, check_vma=False)
```

time: 100 us -> 97 us (0.970)
  Pallas kernels: 96.8 us -> 94.4 us
    pallas_call x1, Pallas kernels: 96.8 us -> 94.4 us  [shards(): pl.pallas_call(kernel, out_shape=jax.ShapeDtypeStruct((BLK, 2048), BF16),...]
where the time goes in v2:
time: 97 us; the launch traced here: 96.7 us
  Pallas kernels  94.4 us (97%)
  local copies, waits for them, and re-layouts  2.3 us (2%)
    pallas_call x1, Pallas kernels, shards(): pl.pallas_call(kernel, out_shape=jax.ShapeDtypeStruct((BLK, 2048), BF16),...  94.4 us
    unnamed x1, local copies, waits for them, and re-layouts  2.3 us

profile of v2, /device:TPU:16, one launch (start us, length us, event | category | flops | bytes accessed | tf_op | source)
XLA Modules:
  0.0 96.7 jit_solution(16178386129397345065)
XLA Ops:
  0.0 94.4 %shard_map.46 = bf16[256,2048]{1,0:T(8,128)(2,1)} custom-call(bf16[256,2176]{1,0:T(8,128)(2,1)} %proj.1, f32[3,2176]{1,0:T(4,128)} %taps.1, bf16[2048,2048]{1,0:T(8,128)(2,1)} %weight.1, bf16[1152,128]{1,0:T(8,128)(2,1)} %constant.2.clone.select), custom_call_target="tpu_custom_call" | custom-call | tf_op jit(solution)/shard_map/pallas_call | solution.py:429
  94.4 2.3 %copy.6 = bf16[256,2048]{1,0:T(8,128)(2,1)} copy(bf16[256,2048]{1,0:T(8,128)(2,1)} %shard_map.46) | data formatting | bytes 2097152

commit v3 on v2

--- a/solution.py
+++ b/solution.py
@@ -20,8 +20,7 @@
 SR, SC = 48, 128
 TILES = 5
 K = 8
-T = BLK // K
-CH = 4 * T
+T, EDGE = 32, 32
 HALF = 1024
 Q0, K0 = 96, 112
 F32, BF16 = jnp.float32, jnp.bfloat16
@@ -193,16 +192,20 @@
         totals[b] = jnp.concatenate([dot_nt(ones, phi), jnp.zeros((8, DV - FP), F32)], axis=1)
 
     feature = lax.broadcasted_iota(jnp.int32, (FS, 128), 0)
-    mine_rows = pl.ds(pl.multiple_of(lax.rem(c, 4) * SR, SR), SR)
-    mine_cols = pl.ds(pl.multiple_of(lax.div(c, 4) * SC, SC), SC)
+
+    def share(o):
+        tile, part_of = lax.rem(lax.div(o, 2), 4), 2 * lax.div(o, 8) + lax.rem(o, 2)
+        return (
+            pl.ds(pl.multiple_of(part_of * SR, SR), SR),
+            pl.ds(pl.multiple_of(tile * SC, SC), SC),
+        )
+
+    mine_rows, mine_cols = share(c)
 
     def to_owner(o, source):
-        return pltpu.make_async_remote_copy(
-            mine.at[
-                ROWS,
-                pl.ds(pl.multiple_of(lax.rem(o, 4) * SR, SR), SR),
-                pl.ds(pl.multiple_of(lax.div(o, 4) * SC, SC), SC),
-            ],
+        rows, cols = share(o)
+        return pltpu.make_async_remote_copy(
+            mine.at[ROWS, rows, cols],
             z1.at[source],
             z1s.at[o],
             z1r.at[source],
@@ -217,22 +220,6 @@
 
     def other(i):
         return lax.rem(c + i, CTX)
-
-    def own_share():
-        @pl.loop(1, CTX)
-        def _(i):
-            to_owner(c, other(i)).wait_recv()
-
-        run = jnp.zeros((SR, SC), F32)
-        for i in range(CTX):
-            z2[i] = run.astype(BF16)
-            run = run + z1[i].astype(F32)
-
-        @pl.loop(1, CTX)
-        def _(i):
-            from_owner(other(i), c).start()
-
-        outer[mine_rows, mine_cols] = z2[c]
 
     outer[FS:, :] = jnp.zeros((FP - FS, DV), BF16)
 
@@ -256,7 +243,7 @@
 
         mine[ROWS, :, cols] = inner[...].astype(BF16)
         for i in range(4):
-            o = j * 4 + i
+            o = 2 * j + 8 * (i // 2) + i % 2
 
             @pl.when(o != c)
             def _():
@@ -266,20 +253,12 @@
             def _():
                 z1[c] = mine[ROWS, mine_rows, mine_cols]
 
-        @pl.when(lax.div(c, 4) == j - 1)
-        def _():
-            own_share()
-
     causal = lax.broadcasted_iota(jnp.int32, (BLK, BLK), 0) >= lax.broadcasted_iota(
         jnp.int32, (BLK, BLK), 1
     )
 
     @pl.loop(0, ROWS)
     def _(b):
-        @pl.when(jnp.logical_and(b == 2, lax.div(c, 4) == 3))
-        def _():
-            own_share()
-
         rows = pl.ds(pl.multiple_of(b * BLK, BLK), BLK)
         qk = gated[rows, DV:]
         value = gated[rows, :DV]
@@ -297,6 +276,21 @@
 
     @pl.loop(1, CTX)
     def _(i):
+        to_owner(c, other(i)).wait_recv()
+
+    run = jnp.zeros((SR, SC), F32)
+    for i in range(CTX):
+        z2[i] = run.astype(BF16)
+        run = run + z1[i].astype(F32)
+
+    @pl.loop(1, CTX)
+    def _(i):
+        from_owner(other(i), c).start()
+
+    outer[mine_rows, mine_cols] = z2[c]
+
+    @pl.loop(1, CTX)
+    def _(i):
         from_owner(c, other(i)).wait_recv()
 
     load_w.wait()
@@ -304,99 +298,99 @@
     def head(by):
         return pl.ds(pl.multiple_of(lax.rem(h + by, ROWS) * DV, DV), DV)
 
-    def ag(k, which):
-        rows, of, to = (
-            (pl.ds(0, CH), 0, 1),
-            (pl.ds(0, CH), 0, 3),
-            (pl.ds(0, CH // 2), 3, 1),
-            (pl.ds(CH // 2, CH // 2), 1, 3),
+    def begin(k):
+        return jnp.where(k == K - 1, BLK - EDGE, jnp.maximum(k * T - (T - EDGE), 0))
+
+    def tokens(k, n):
+        return pl.ds(pl.multiple_of(begin(k), EDGE), n)
+
+    def chunk(k, first, n):
+        return pl.ds(pl.multiple_of(begin(k) * 4 + first, EDGE), n)
+
+    def ag(k, n, which):
+        first, size, of, to = ((0, 4 * n, 0, 1), (0, 4 * n, 0, 3), (0, 2 * n, 3, 1), (2 * n, 2 * n, 1, 3))[which]
+        ref = att.at[chunk(k, first, size), head(of)]
+        return pltpu.make_async_remote_copy(ref, ref, ags.at[k, which], agr.at[k, which], row(to), MESH)
+
+    def rs(k, n, which):
+        a, b, t = pl.ds(0, HALF), pl.ds(HALF, HALF), tokens(k, n)
+        j, cols, to_ref, to = (
+            (2, a, opp.at[0, t], right),
+            (2, b, opp.at[1, t], left),
+            (1, b, left_in.at[t, b], right),
+            (3, a, right_in.at[t, a], left),
+            (1, a, left_in.at[t, a], right),
+            (3, b, right_in.at[t, b], left),
         )[which]
         return pltpu.make_async_remote_copy(
-            att.at[k, rows, head(of)],
-            att.at[k, rows, head(of)],
-            ags.at[k, which],
-            agr.at[k, which],
-            row(to),
-            MESH,
-        )
-
-    def rs(k, which):
-        a, b = pl.ds(0, HALF), pl.ds(HALF, HALF)
-        j, cols, land, to = (
-            (2, a, opp.at[k, 0], right),
-            (2, b, opp.at[k, 1], left),
-            (1, b, left_in.at[k, :, b], right),
-            (3, a, right_in.at[k, :, a], left),
-            (1, a, left_in.at[k, :, a], right),
-            (3, b, right_in.at[k, :, b], left),
-        )[which]
-        return pltpu.make_async_remote_copy(
-            part.at[k, pl.ds(j * T, T), cols], land, rss.at[k, which], rsr.at[k, which], to, MESH
+            part.at[chunk(k, j * n, n), cols], to_ref, rss.at[k, which], rsr.at[k, which], to, MESH
         )
 
     outer_total = outer[PHI : PHI + 1, :FP].astype(F32)
+
+    def attend(k, n):
+        places = [
+            pl.ds(pl.multiple_of(lax.rem(g + j, ROWS) * BLK + begin(k), EDGE), n) for j in range(4)
+        ]
+        phi = jnp.concatenate([phiq[place, :] for place in places], axis=0)
+        top = jnp.concatenate([num[place, :] for place in places], axis=0) + dot(phi, outer[...])
+        bottom = jnp.concatenate([den[place, :] for place in places], axis=0)[:, 0:1] + jnp.sum(
+            phi.astype(F32) * outer_total, axis=1, keepdims=True
+        )
+        att[chunk(k, 0, 4 * n), head(0)] = (top / bottom).astype(BF16)
+        ag(k, n, 0).start()
+        ag(k, n, 1).start()
+
+    def forward(k, n):
+        ag(k, n, 0).wait_recv()
+        ag(k, n, 2).start()
+        ag(k, n, 1).wait_recv()
+        ag(k, n, 3).start()
+
+    def project(k, n):
+        ag(k, n, 2).wait_recv()
+        ag(k, n, 3).wait_recv()
+        for half in range(2):
+            for m in range(2):
+                cols = slice(half * HALF + m * 512, half * HALF + m * 512 + 512)
+                p = dot(att[chunk(k, 0, 4 * n), :], w[:, cols])
+                own[tokens(k, n), cols] = p[:n]
+                part[chunk(k, n, 3 * n), cols] = p[n:].astype(BF16)
+            for which in ((0, 3), (1, 2))[half]:
+                rs(k, n, which).start()
+
+    def join(k, n):
+        for side, j, cols in ((0, 1, slice(0, HALF)), (1, 3, slice(HALF, 2 * HALF))):
+            rs(k, n, side).wait_recv()
+            rows = chunk(k, j * n, n)
+            both = part[rows, cols].astype(F32) + opp[side, tokens(k, n), :].astype(F32)
+            part[rows, cols] = both.astype(BF16)
+            rs(k, n, 4 + side).start()
+
+    def finish(k, n):
+        for which in range(2, 6):
+            rs(k, n, which).wait_recv()
+        t = tokens(k, n)
+        out[t, :] = (own[t, :] + left_in[t, :].astype(F32) + right_in[t, :].astype(F32)).astype(BF16)
+
+    def sized(k, stage):
+        edge = jnp.logical_or(k == 0, k == K - 1)
+
+        @pl.when(edge)
+        def _():
+            stage(k, EDGE)
+
+        @pl.when(jnp.logical_not(edge))
+        def _():
+            stage(k, T)
 
     @pl.loop(0, K + 4)
     def _(step):
-        @pl.when(step < K)
-        def _():
-            k = step
-            places = [
-                pl.ds(pl.multiple_of(lax.rem(g + j, ROWS) * BLK + k * T, T), T) for j in range(4)
-            ]
-            phi = jnp.concatenate([phiq[place, :] for place in places], axis=0)
-            top = jnp.concatenate([num[place, :] for place in places], axis=0) + dot(phi, outer[...])
-            bottom = jnp.concatenate([den[place, :] for place in places], axis=0)[:, 0:1] + jnp.sum(
-                phi.astype(F32) * outer_total, axis=1, keepdims=True
-            )
-            att[k, :, head(0)] = (top / bottom).astype(BF16)
-            ag(k, 0).start()
-            ag(k, 1).start()
-
-        @pl.when(jnp.logical_and(step >= 1, step < K + 1))
-        def _():
-            k = step - 1
-            ag(k, 0).wait_recv()
-            ag(k, 2).start()
-            ag(k, 1).wait_recv()
-            ag(k, 3).start()
-
-        @pl.when(jnp.logical_and(step >= 2, step < K + 2))
-        def _():
-            k = step - 2
-            ag(k, 2).wait_recv()
-            ag(k, 3).wait_recv()
-            for half in range(2):
-                for n in range(2):
-                    cols = slice(half * HALF + n * 512, half * HALF + n * 512 + 512)
-                    p = dot(att[k], w[:, cols])
-                    own[k, :, cols] = p[:T]
-                    part[k, T:, cols] = p[T:].astype(BF16)
-                for which in ((0, 3), (1, 2))[half]:
-                    rs(k, which).start()
-
-        @pl.when(jnp.logical_and(step >= 3, step < K + 3))
-        def _():
-            k = step - 3
-            rs(k, 0).wait_recv()
-            part[k, T : 2 * T, :HALF] = (
-                part[k, T : 2 * T, :HALF].astype(F32) + opp[k, 0].astype(F32)
-            ).astype(BF16)
-            rs(k, 4).start()
-            rs(k, 1).wait_recv()
-            part[k, 3 * T :, HALF:] = (
-                part[k, 3 * T :, HALF:].astype(F32) + opp[k, 1].astype(F32)
-            ).astype(BF16)
-            rs(k, 5).start()
-
-        @pl.when(step >= 4)
-        def _():
-            k = step - 4
-            for which in range(2, 6):
-                rs(k, which).wait_recv()
-            out[pl.ds(pl.multiple_of(k * T, T), T), :] = (
-                own[k] + left_in[k].astype(F32) + right_in[k].astype(F32)
-            ).astype(BF16)
+        for late, stage in enumerate((attend, forward, project, join, finish)):
+
+            @pl.when(jnp.logical_and(step >= late, step < K + late))
+            def _():
+                sized(step - late, stage)
 
     for i in (1, 2, 3):
         send_keys(i).wait_send()
@@ -413,12 +407,15 @@
         to_owner(other(i), c).wait_send()
         from_owner(other(i), c).wait_send()
 
+    def sent(k, n):
+        for which in range(4):
+            ag(k, n, which).wait_send()
+        for which in range(6):
+            rs(k, n, which).wait_send()
+
     @pl.loop(0, K)
     def _(k):
-        for which in range(4):
-            ag(k, which).wait_send()
-        for which in range(6):
-            rs(k, which).wait_send()
+        sized(k, sent)
 
 
 def shards(projected, conv_taps, out_weight):
@@ -450,12 +447,12 @@
             pltpu.VMEM((CTX, SR, SC), BF16),
             pltpu.VMEM((FP, DV), BF16),
             pltpu.VMEM((2048, 2048), BF16),
-            pltpu.VMEM((K, CH, 2048), BF16),
-            pltpu.VMEM((K, CH, 2048), BF16),
-            pltpu.VMEM((K, T, 2048), F32),
-            pltpu.VMEM((K, 2, T, HALF), BF16),
-            pltpu.VMEM((K, T, 2048), BF16),
-            pltpu.VMEM((K, T, 2048), BF16),
+            pltpu.VMEM((TOK, 2048), BF16),
+            pltpu.VMEM((TOK, 2048), BF16),
+            pltpu.VMEM((BLK, 2048), F32),
+            pltpu.VMEM((2, BLK, HALF), BF16),
+            pltpu.VMEM((BLK, 2048), BF16),
+            pltpu.VMEM((BLK, 2048), BF16),
             dma,
             dma((4, TILES)),
             dma((4, TILES)),

time: 97 us -> 92.1 us (0.949)
  Pallas kernels: 94.4 us -> 89.7 us
    pallas_call x1, Pallas kernels: 94.4 us -> 89.7 us  [shards(): pl.pallas_call(kernel, out_shape=jax.ShapeDtypeStruct((BLK, 2048), BF16),...]
where the time goes in v3:
time: 92.1 us; the launch traced here: 92 us
  Pallas kernels  89.7 us (97%)
  local copies, waits for them, and re-layouts  2.3 us (2%)
    pallas_call x1, Pallas kernels, shards(): pl.pallas_call(kernel, out_shape=jax.ShapeDtypeStruct((BLK, 2048), BF16),...  89.7 us
    unnamed x1, local copies, waits for them, and re-layouts  2.3 us

profile of v3, /device:TPU:16, one launch (start us, length us, event | category | flops | bytes accessed | tf_op | source)
XLA Modules:
  0.0 92.0 jit_solution(17384911566466549578)
XLA Ops:
  0.0 89.7 %shard_map.46 = bf16[256,2048]{1,0:T(8,128)(2,1)} custom-call(bf16[256,2176]{1,0:T(8,128)(2,1)} %proj.1, f32[3,2176]{1,0:T(4,128)} %taps.1, bf16[2048,2048]{1,0:T(8,128)(2,1)} %weight.1, bf16[1152,128]{1,0:T(8,128)(2,1)} %constant.2.clone.select), custom_call_target="tpu_custom_call" | custom-call | tf_op jit(solution)/shard_map/pallas_call | solution.py:426
  89.7 2.3 %copy.6 = bf16[256,2048]{1,0:T(8,128)(2,1)} copy(bf16[256,2048]{1,0:T(8,128)(2,1)} %shard_map.46) | data formatting | bytes 2097152

commit v4 on v3

--- a/solution.py
+++ b/solution.py
@@ -384,9 +384,9 @@
         def _():
             stage(k, T)
 
-    @pl.loop(0, K + 4)
+    @pl.loop(0, K + 5)
     def _(step):
-        for late, stage in enumerate((attend, forward, project, join, finish)):
+        for stage, late in ((attend, 0), (forward, 1), (project, 2), (join, 3), (finish, 5)):
 
             @pl.when(jnp.logical_and(step >= late, step < K + late))
             def _():

time: 92.1 us -> 90.7 us (0.985)
  Pallas kernels: 89.7 us -> 88.2 us
    pallas_call x1, Pallas kernels: 89.7 us -> 88.2 us  [shards(): pl.pallas_call(kernel, out_shape=jax.ShapeDtypeStruct((BLK, 2048), BF16),...]
where the time goes in v4:
time: 90.7 us; the launch traced here: 90.5 us
  Pallas kernels  88.2 us (97%)
  local copies, waits for them, and re-layouts  2.3 us (3%)
    pallas_call x1, Pallas kernels, shards(): pl.pallas_call(kernel, out_shape=jax.ShapeDtypeStruct((BLK, 2048), BF16),...  88.2 us
    unnamed x1, local copies, waits for them, and re-layouts  2.3 us

profile of v4, /device:TPU:16, one launch (start us, length us, event | category | flops | bytes accessed | tf_op | source)
XLA Modules:
  0.0 90.5 jit_solution(5371463511726536034)
XLA Ops:
  0.0 88.2 %shard_map.46 = bf16[256,2048]{1,0:T(8,128)(2,1)} custom-call(bf16[256,2176]{1,0:T(8,128)(2,1)} %proj.1, f32[3,2176]{1,0:T(4,128)} %taps.1, bf16[2048,2048]{1,0:T(8,128)(2,1)} %weight.1, bf16[1152,128]{1,0:T(8,128)(2,1)} %constant.2.clone.select), custom_call_target="tpu_custom_call" | custom-call | tf_op jit(solution)/shard_map/pallas_call | solution.py:426
  88.2 2.3 %copy.6 = bf16[256,2048]{1,0:T(8,128)(2,1)} copy(bf16[256,2048]{1,0:T(8,128)(2,1)} %shard_map.46) | data formatting | bytes 2097152

commit v5 on v4

--- a/solution.py
+++ b/solution.py
@@ -58,10 +58,10 @@
 
 
 def kernel(
-    proj, taps, weight, select, out,
-    x, packed, quarter, raw, land, tap, gated, phik, totals, num, den, phiq,
+    proj, taps_in, weight, select_in, out_to,
+    x, taps, select, out, packed, quarter, raw, land, tap, gated, phik, totals, num, den, phiq,
     inner, mine, z1, z2, outer, w, att, part, own, opp, left_in, right_in,
-    ps, xs, xr, ts, tr, ws, z1s, z1r, z2s, z2r, ags, agr, rss, rsr,
+    ps, os, xs, xr, ts, tr, ws, z1s, z1r, z2s, z2r, ags, agr, rss, rsr,
 ):
     c, h, g = lax.axis_index("ctx"), lax.axis_index("row"), lax.axis_index("col")
 
@@ -74,8 +74,12 @@
     right, left = at("col", g, 1, 4), at("col", g, 3, 4)
     sends_tail = jnp.logical_and(h == ROWS - 1, c < CTX - 1)
 
-    load_x = pltpu.make_async_copy(proj, x, ps)
+    load_x = pltpu.make_async_copy(proj, x, ps.at[0])
     load_x.start()
+    load_taps = pltpu.make_async_copy(taps_in, taps, ps.at[1])
+    load_taps.start()
+    load_select = pltpu.make_async_copy(select_in, select, ps.at[2])
+    load_select.start()
     load_w = pltpu.make_async_copy(weight, w, ws)
     load_w.start()
 
@@ -112,6 +116,7 @@
             part_i = pltpu.roll(last[i * 64 : i * 64 + 64], 32 * (i + 1) % 128, 1)
             q = jnp.where(lane_q // 32 == i, part_i, q)
         quarter[head] = q.astype(BF16)
+    load_taps.wait()
     window = taps[:, pl.ds(pl.multiple_of(h * DV, DV), WIN)]
     window = jnp.concatenate([window, jnp.zeros((5, WIN), F32)], axis=0)
     tap[...] = pltpu.roll(window, WIN - 2 * FEAT * (h + 1), 1)
@@ -180,6 +185,7 @@
         return (v * (t[0] * v + t[1] * pltpu.roll(v, 1, 0) + t[2] * pltpu.roll(v, 2, 0)))[16:]
 
     ones = jnp.ones((8, BLK), BF16)
+    load_select.wait()
     k1, k2, q1, q2 = (select[i * FP : i * FP + FP] for i in range(4))
     move = select[4 * FP :]
 
@@ -367,11 +373,15 @@
             part[rows, cols] = both.astype(BF16)
             rs(k, n, 4 + side).start()
 
+    def store(k, n):
+        return pltpu.make_async_copy(out.at[tokens(k, n)], out_to.at[tokens(k, n)], os.at[k])
+
     def finish(k, n):
         for which in range(2, 6):
             rs(k, n, which).wait_recv()
         t = tokens(k, n)
         out[t, :] = (own[t, :] + left_in[t, :].astype(F32) + right_in[t, :].astype(F32)).astype(BF16)
+        store(k, n).start()
 
     def sized(k, stage):
         edge = jnp.logical_or(k == 0, k == K - 1)
@@ -412,6 +422,7 @@
             ag(k, n, which).wait_send()
         for which in range(6):
             rs(k, n, which).wait_send()
+        store(k, n).wait()
 
     @pl.loop(0, K)
     def _(k):
@@ -420,16 +431,18 @@
 
 def shards(projected, conv_taps, out_weight):
     select = jnp.asarray(selectors(), BF16)
-    vmem = pl.BlockSpec(memory_space=pltpu.VMEM)
     hbm = pl.BlockSpec(memory_space=pl.ANY)
     dma = pltpu.SemaphoreType.DMA
     return pl.pallas_call(
         kernel,
         out_shape=jax.ShapeDtypeStruct((BLK, 2048), BF16),
-        in_specs=[hbm, vmem, hbm, vmem],
-        out_specs=vmem,
+        in_specs=[hbm] * 4,
+        out_specs=hbm,
         scratch_shapes=[
             pltpu.VMEM((BLK, ROWS * (2 * FEAT + DV)), BF16),
+            pltpu.VMEM((3, ROWS * (2 * FEAT + DV)), F32),
+            pltpu.VMEM((4 * FP + 128, 128), BF16),
+            pltpu.VMEM((BLK, 2048), BF16),
             pltpu.VMEM((ROWS, TILES, BLK, 128), BF16),
             pltpu.VMEM((ROWS, BLK // 4, 128), BF16),
             pltpu.VMEM((TILES, 16 + TOK, 128), BF16),
@@ -453,7 +466,8 @@
             pltpu.VMEM((2, BLK, HALF), BF16),
             pltpu.VMEM((BLK, 2048), BF16),
             pltpu.VMEM((BLK, 2048), BF16),
-            dma,
+            dma((3,)),
+            dma((K,)),
             dma((4, TILES)),
             dma((4, TILES)),
             dma((4,)),

time: 90.7 us -> 89.2 us (0.983)
  Pallas kernels: 88.2 us -> 86.7 us
    pallas_call x1, Pallas kernels: 88.2 us -> 86.7 us  [shards(): pl.pallas_call(kernel, out_shape=jax.ShapeDtypeStruct((BLK, 2048), BF16),...]
where the time goes in v5:
time: 89.2 us; the launch traced here: 89 us
  Pallas kernels  86.7 us (97%)
  local copies, waits for them, and re-layouts  2.3 us (3%)
    pallas_call x1, Pallas kernels, shards(): pl.pallas_call(kernel, out_shape=jax.ShapeDtypeStruct((BLK, 2048), BF16),...  86.7 us
    unnamed x1, local copies, waits for them, and re-layouts  2.3 us

profile of v5, /device:TPU:16, one launch (start us, length us, event | category | flops | bytes accessed | tf_op | source)
XLA Modules:
  0.0 89.0 jit_solution(6921726946017777037)
XLA Ops:
  0.0 86.7 %shard_map.46 = bf16[256,2048]{1,0:T(8,128)(2,1)} custom-call(bf16[256,2176]{1,0:T(8,128)(2,1)} %proj.1, f32[3,2176]{1,0:T(4,128)} %taps_in.1, bf16[2048,2048]{1,0:T(8,128)(2,1)} %weight.1, bf16[1152,128]{1,0:T(8,128)(2,1)} %constant.2.clone.select_in), custom_call_target="tpu_custom_call" | custom-call | tf_op jit(solution)/shard_map/pallas_call | solution.py:436
  86.7 2.3 %copy.6 = bf16[256,2048]{1,0:T(8,128)(2,1)} copy(bf16[256,2048]{1,0:T(8,128)(2,1)} %shard_map.46) | data formatting | bytes 2097152

commit v6 on v5

--- a/solution.py
+++ b/solution.py
@@ -19,8 +19,8 @@
 FS = 192
 SR, SC = 48, 128
 TILES = 5
-K = 8
-T, EDGE = 32, 32
+K = 9
+T, EDGE = 32, 16
 HALF = 1024
 Q0, K0 = 96, 112
 F32, BF16 = jnp.float32, jnp.bfloat16

time: 89.2 us -> 89.8 us (level)
  no operation moved by 1% of the time
where the time goes in v6:
time: 89.8 us; the launch traced here: 89.4 us
  Pallas kernels  87.1 us (97%)
  local copies, waits for them, and re-layouts  2.3 us (3%)
    pallas_call x1, Pallas kernels, shards(): pl.pallas_call(kernel, out_shape=jax.ShapeDtypeStruct((BLK, 2048), BF16),...  87.1 us
    unnamed x1, local copies, waits for them, and re-layouts  2.3 us

profile of v6, /device:TPU:16, one launch (start us, length us, event | category | flops | bytes accessed | tf_op | source)
XLA Modules:
  0.0 89.4 jit_solution(12006306620469273155)
XLA Ops:
  0.0 87.1 %shard_map.46 = bf16[256,2048]{1,0:T(8,128)(2,1)} custom-call(bf16[256,2176]{1,0:T(8,128)(2,1)} %proj.1, f32[3,2176]{1,0:T(4,128)} %taps_in.1, bf16[2048,2048]{1,0:T(8,128)(2,1)} %weight.1, bf16[1152,128]{1,0:T(8,128)(2,1)} %constant.2.clone.select_in), custom_call_target="tpu_custom_call" | custom-call | tf_op jit(solution)/shard_map/pallas_call | solution.py:436
  87.1 2.3 %copy.6 = bf16[256,2048]{1,0:T(8,128)(2,1)} copy(bf16[256,2048]{1,0:T(8,128)(2,1)} %shard_map.46) | data formatting | bytes 2097152
